TPU v7x, 32 devices: a whole 2x2x4 slice. The times are simulated.
32 devices in a mesh: dp: 8 (over z, y), fsdp: 4 (over x, core).
Axes of the slice: x: 2, y: 2, z: 4, core: 2. Of those that a mesh axis runs over, the one named last changes fastest.
Arguments:
- features: bfloat16 [8, 4, 18, 180, 300], P('dp', 'fsdp'), may hold values from -8 to 8
- land_mask: int32 [144, 180], replicated, may hold values from 0 to 1, as said below
- cotangent: bfloat16 [8, 4, 18, 180, 300], P('dp', 'fsdp'), may hold values from -6 to 6
- kernel: bfloat16 [300, 49], P('fsdp'), may hold values from -0.875 to 0.875
- norm_gain: bfloat16 [300], P('fsdp'), may hold values from 0.099609375 to 1.8984375
- norm_shift: bfloat16 [300], P('fsdp'), may hold values from -3 to 3
- in_proj: bfloat16 [300, 1200], P('fsdp'), may hold values from -0.375 to 0.375
- in_bias: bfloat16 [1200], P('fsdp'), may hold values from -3 to 3
- out_proj: bfloat16 [1200, 300], P('fsdp'), may hold values from -0.1875 to 0.1875
- out_bias: bfloat16 [300], P('fsdp'), may hold values from -3 to 3
Outputs:
- output: bfloat16 [8, 4, 18, 180, 300], P('dp', 'fsdp')
- grad_features: bfloat16 [8, 4, 18, 180, 300], P('dp', 'fsdp')
- grad_kernel: float32 [300, 49], P('fsdp')
- grad_gain: float32 [300], P('fsdp')
- grad_shift: float32 [300], P('fsdp')
- grad_in_proj: float32 [300, 1200], P('fsdp')
- grad_in_bias: float32 [1200], P('fsdp')
- grad_out_proj: float32 [1200, 300], P('fsdp')
- grad_out_bias: float32 [300], P('fsdp')
Inputs may be any that keep to these rules, and one draw needn't show every extreme that they name: `land_mask`: 1 marks an ocean cell; every latitude row has ocean cells.
All inputs are finite; a program needn't handle non-finite values.
Results may differ from a plain program's by a relative error of at most 0.0059.
Values may be sent and summed in bfloat16 or wider, within the bound.
No kernel may reach another device: no remote copies, remote signals or barrier semaphores. Data moves between devices by JAX's collectives and lax.ppermute only.
A program may use at most 320 MiB of HBM per device.

v0:
```python
import jax
import jax.numpy as jnp
from jax import lax
from jax.sharding import PartitionSpec as P

KW = 7
TILES = 8


EPSILON = 1e-05


def with_halo(array, sides, width):
    for axis, dim in sides:
        count, length = (lax.axis_size(axis), array.shape[dim])
        up = [(i, (i + 1) % count) for i in range(count - 1)]
        down = [(j, i) for i, j in up]
        last = lax.slice_in_dim(array, length - width, length, axis=dim)
        initial = lax.slice_in_dim(array, 0, width, axis=dim)
        before = lax.ppermute(last, axis, up)
        after = lax.ppermute(initial, axis, down)
        array = jnp.concatenate([before, array, after], axis=dim)
    return array


def convolve_rows(padded, taps, height):
    span = KW // 2
    total = None
    for row_tap in range(KW):
        for col_tap in range(KW):
            term = taps[:, row_tap * KW + col_tap] * jnp.roll(
                padded[:, row_tap : row_tap + height], span - col_tap, axis=2
            )
            total = term if total is None else total + term
    return total


def convolve_back(gpadded, taps, height):
    span = KW // 2
    total = None
    for row_tap in range(KW):
        for col_tap in range(KW):
            start = 2 * span - row_tap
            term = taps[:, row_tap * KW + col_tap] * jnp.roll(
                gpadded[:, start : start + height], col_tap - span, axis=2
            )
            total = term if total is None else total + term
    return total


def kernel_terms(padded, gconv, height):
    span = KW // 2
    gfloat = gconv.astype(jnp.float32)
    columns = []
    for row_tap in range(KW):
        for col_tap in range(KW):
            shifted = jnp.roll(
                padded[:, row_tap : row_tap + height], span - col_tap, axis=2
            ).astype(jnp.float32)
            columns.append(jnp.sum(shifted * gfloat, axis=(0, 1, 2)))
    return jnp.stack(columns, axis=1)


def own_share(value):
    share = value.shape[0] // lax.axis_size("fsdp")
    return lax.dynamic_slice_in_dim(value, lax.axis_index("fsdp") * share, share, 0)


def cut_rims(padded, tile_index, span):
    zero = jnp.zeros((), padded.dtype)
    top = jnp.where(tile_index == 0, zero, padded[:, :span])
    bottom = jnp.where(tile_index == TILES - 1, zero, padded[:, -span:])
    return jnp.concatenate([top, padded[:, span:-span], bottom], axis=1)


def local(
    features,
    land_mask,
    cotangent,
    kernel,
    norm_gain,
    norm_shift,
    in_proj,
    in_bias,
    out_proj,
    out_bias,
):
    feats = features[0]
    samples, height, width, channels = feats.shape
    span = KW // 2
    tile_index = lax.axis_index("dp") % TILES
    local_mask = lax.dynamic_slice_in_dim(land_mask, tile_index * height, height, 0)
    maskf = local_mask.astype(jnp.float32)
    ocean = maskf[None, :, :, None]
    whole = (
        lax.all_gather(kernel, "fsdp", axis=0, tiled=True),
        lax.all_gather(norm_gain, "fsdp", axis=0, tiled=True),
        lax.all_gather(norm_shift, "fsdp", axis=0, tiled=True),
        lax.all_gather(in_proj, "fsdp", axis=0, tiled=True),
        lax.all_gather(in_bias, "fsdp", axis=0, tiled=True),
        lax.all_gather(out_proj, "fsdp", axis=0, tiled=True),
        lax.all_gather(out_bias, "fsdp", axis=0, tiled=True),
    )
    taps = whole[0].astype(jnp.float32)
    gamma = whole[1].astype(jnp.float32)
    betas = whole[2].astype(jnp.float32)
    in_full = whole[3]
    in_b = whole[4].astype(jnp.float32)
    out_full = whole[5]
    out_b = whole[6].astype(jnp.float32)
    masked = feats * local_mask[None, :, :, None].astype(jnp.bfloat16)
    padded = with_halo(masked, (("dp", 1),), span)
    padded = cut_rims(padded, tile_index, span)
    conv_out = convolve_rows(padded, taps, height)
    local_count = samples * jnp.sum(maskf)
    sums, count = lax.psum((jnp.sum(conv_out * ocean, axis=(0, 1, 2)), local_count), ("dp", "fsdp"))
    count = jnp.maximum(count, 1.0)
    centered = conv_out - sums / count
    spread = lax.psum(jnp.sum(ocean * centered * centered, axis=(0, 1, 2)), ("dp", "fsdp"))
    inverse = lax.rsqrt(spread / count + EPSILON)
    normed = centered * inverse
    zrows = (gamma * normed + betas).astype(jnp.bfloat16).reshape(-1, channels)
    hidden = jnp.dot(zrows, in_full, preferred_element_type=jnp.float32) + in_b
    act, gelu_pull = jax.vjp(jax.nn.gelu, hidden)
    act_low = act.astype(jnp.bfloat16)
    branch = jnp.dot(act_low, out_full, preferred_element_type=jnp.float32) + out_b
    output = ((feats.astype(jnp.float32) + branch.reshape(feats.shape)) * ocean).astype(
        jnp.bfloat16
    )
    again = (
        lax.all_gather(norm_gain, "fsdp", axis=0, tiled=True),
        lax.all_gather(in_proj, "fsdp", axis=0, tiled=True),
        lax.all_gather(out_proj, "fsdp", axis=0, tiled=True),
    )
    gamma_back = again[0].astype(jnp.float32)
    in_back = again[1]
    out_back = again[2]
    gout = cotangent[0].astype(jnp.float32) * ocean
    gbranch = gout.reshape(-1, channels).astype(jnp.bfloat16)
    contract_rows = (((0,), (0,)), ((), ()))
    contract_cols = (((1,), (1,)), ((), ()))
    grad_out_w = lax.dot_general(
        act_low, gbranch, contract_rows, preferred_element_type=jnp.float32
    )
    grad_out_b = jnp.sum(gbranch.astype(jnp.float32), axis=0)
    gact = lax.dot_general(gbranch, out_back, contract_cols, preferred_element_type=jnp.float32)
    ghidden = gelu_pull(gact)[0].astype(jnp.bfloat16)
    grad_in_w = lax.dot_general(zrows, ghidden, contract_rows, preferred_element_type=jnp.float32)
    grad_in_b = jnp.sum(ghidden.astype(jnp.float32), axis=0)
    gz_rows = lax.dot_general(ghidden, in_back, contract_cols, preferred_element_type=jnp.float32)
    normed_rows = normed.reshape(-1, channels)
    grad_gamma, grad_beta = lax.psum(
        (jnp.sum(gz_rows * normed_rows, axis=0), jnp.sum(gz_rows, axis=0)), ("dp", "fsdp")
    )
    gzvals = gz_rows.reshape(feats.shape)
    gconv = (
        inverse
        * (gamma_back * gzvals - ocean * gamma_back * (grad_beta + normed * grad_gamma) / count)
    ).astype(jnp.bfloat16)
    gpadded = with_halo(gconv, (("dp", 1),), span)
    gpadded = cut_rims(gpadded, tile_index, span)
    gmasked = convolve_back(gpadded, taps, height)
    grad_features = (gout + ocean * gmasked).astype(jnp.bfloat16)
    grad_taps = kernel_terms(padded, gconv, height)
    local_grads = (grad_taps, grad_in_w, grad_in_b, grad_out_w, grad_out_b)
    totals = lax.psum(
        (local_grads[0], local_grads[1], local_grads[2], local_grads[3], local_grads[4]),
        ("dp", "fsdp"),
    )
    shares = tuple((own_share(value) for value in totals))
    return (
        output[None],
        grad_features[None],
        shares[0],
        own_share(grad_gamma),
        own_share(grad_beta),
        shares[1],
        shares[2],
        shares[3],
        shares[4],
    )


def solution(mesh):
    placed = (
        P("dp", "fsdp", None, None, None),
        P(),
        P("dp", "fsdp", None, None, None),
        P("fsdp", None),
        P("fsdp"),
        P("fsdp"),
        P("fsdp", None),
        P("fsdp"),
        P("fsdp", None),
        P("fsdp"),
    )
    return jax.shard_map(
        local,
        mesh=mesh,
        in_specs=placed,
        out_specs=(
            P("dp", "fsdp", None, None, None),
            P("dp", "fsdp", None, None, None),
            P("fsdp", None),
            P("fsdp"),
            P("fsdp"),
            P("fsdp", None),
            P("fsdp"),
            P("fsdp", None),
            P("fsdp"),
        ),
        check_vma=False,
    )
```

profile of v0, /device:TPU:0, one launch (start us, length us, event | category | flops | bytes accessed | tf_op | source)
XLA Modules:
  0.0 744.1 jit_solution(17400012117220363214)
XLA Ops:
  28.6 7.2 all-reduce.8
  36.4 8.0 %all-gather.1 = bf16[4,75,1200]{2,1,0:T(8,128)(2,1)S(1)} all-gather(bf16[1,75,1200]{2,1,0:T(8,128)(2,1)} %bitcast.32), channel_id=1, replica_groups=mesh['dp'=8,'fsdp'=4] {'fsdp'}, dimensions={0}, use_global_device_ids=true | all-gather | bytes 900000 | tf_op jit(solution)/shard_map/all_gather | solution.py:99
  50.8 9.7 %all-gather.2 = bf16[4,300,300]{2,1,0:T(8,128)(2,1)S(1)} all-gather(bf16[1,300,300]{2,1,0:T(8,128)(2,1)} %bitcast.31), channel_id=1, replica_groups=mesh['dp'=8,'fsdp'=4] {'fsdp'}, dimensions={0}, use_global_device_ids=true | all-gather | bytes 900000 | tf_op jit(solution)/shard_map/all_gather | solution.py:101
  69.2 7.3 fusion.154
  76.5 7.1 fusion.155
  83.6 7.2 fusion.156
  90.7 10.1 %fusion.134 = (bf16[1,18,178,300]{3,2,1,0:T(8,128)(2,1)}, bf16[1,18,178,300]{3,2,1,0:T(8,128)(2,1)}, bf16[1,18,178,300]{3,2,1,0:T(8,128)(2,1)}, bf16[1,18,178,30...) fusion(bf16[1,3,180,300]{3,2,1,0:T(8,128)(2,1)S(1)} %get-tuple-, ...), kind=kLoop, calls=%fused_computation.400 | loop fusion | flops 5767200 | bytes 18967968 | tf_op jit(solution)/shard_map/concatenate | solution.py:73
  100.9 10.2 %fusion.135 = (bf16[1,18,179,300]{3,2,1,0:T(8,128)(2,1)}, bf16[1,18,179,300]{3,2,1,0:T(8,128)(2,1)}, bf16[1,18,179,300]{3,2,1,0:T(8,128)(2,1)}, bf16[1,18,179,30...) fusion(bf16[1,3,180,300]{3,2,1,0:T(8,128)(2,1)S(1)} %get-tuple-, ...), kind=kLoop, calls=%fused_computation.401 | loop fusion | flops 5799600 | bytes 19043568 | tf_op jit(solution)/shard_map/concatenate | solution.py:73
  111.0 10.0 %fusion.133 = (bf16[1,18,177,300]{3,2,1,0:T(8,128)(2,1)}, bf16[1,18,177,300]{3,2,1,0:T(8,128)(2,1)}, bf16[1,18,177,300]{3,2,1,0:T(8,128)(2,1)}, bf16[1,18,177,30...) fusion(bf16[1,3,180,300]{3,2,1,0:T(8,128)(2,1)S(1)} %get-tuple-, ...), kind=kLoop, calls=%fused_computation.399 | loop fusion | flops 5734800 | bytes 18892368 | tf_op jit(solution)/shard_map/concatenate | solution.py:73
  122.7 78.0 %multiply_reduce_fusion = (f32[300]{0:T(512)S(1)}, f32[1,18,180,300]{3,2,1,0:T(8,128)}) fusion(f32[18,180]{1,0:T(8,128)S(1)} %get-tuple-element.126, bf16[1,3,180,300]{3,2,1,0:T(8,128)(2,1)S(1)} %get-tuple-element.302, bf16[1,18,180,300]{3,2,1,0:T(8,128)(2,1)S(1)} %bitcast_multiply_fusion, bf16[1,18,177,300]{3,2,1,0:T(8,128)(2,1)} %get-tuple-element.238, ...), kind=kLoop, calls=%fused_computation.394 | loop fusion | flops 291599712 | bytes 88071360 | tf_op jit(solution)/shard_map/reduce_sum | solution.py:116
  200.8 41.7 %all-reduce.6 = (f32[300]{0:T(512)S(1)}, f32[]{:T(128)}) all-reduce(f32[300]{0:T(512)S(1)} %get-tuple-element.127, f32[]{:T(128)} %get-tuple-element.125), channel_id=1, replica_groups=mesh['dp'=8,'fsdp'=4] {'dp','fsdp'}, use_global_device_ids=true, to_apply=%region_1.2 | all-reduce | flops 301 | bytes 2408 | tf_op jit(solution)/shard_map/psum | solution.py:116
  246.1 41.2 %psum.72 = f32[300]{0:T(512)S(1)} all-reduce(f32[300]{0:T(512)S(1)} %fusion.55), channel_id=1, replica_groups=mesh['dp'=8,'fsdp'=4] {'dp','fsdp'}, use_global_device_ids=true, to_apply=%region_5.6 | all-reduce | flops 300 | bytes 2400 | tf_op jit(solution)/shard_map/psum | solution.py:119
  295.4 14.4 %multiply_convert_fusion = (bf16[3240,1200]{0,1:T(8,128)(2,1)}, f32[3240,1200]{0,1:T(8,128)}) fusion(f32[1200]{0:T(1024)S(1)} %copy-done.119, bf16[3240,300]{1,0:T(8,128)(2,1)} %reshape.3661, bf16[300,1200]{1,0:T(8,128)(2,1)} %reshape.3682), kind=kOutput, calls=%fused_computation.211 | convolution fusion | flops 2371681280 | bytes 25996800 | tf_op jit(solution)/shard_map/dot_general | solution.py:123
  309.9 18.4 %convert_reduce_fusion = (f32[1200]{0:T(1024)}, bf16[3240,1200]{0,1:T(8,128)(2,1)S(1)}) fusion(f32[3240,1200]{0,1:T(8,128)} %get-tuple-element.298, bf16[1200,300]{1,0:T(8,128)(2,1)S(1)} %copy-done.26, f32[3240,300]{1,0:T(8,128)} %reshape.3666, f32[3240]{0:T(1024)S(1)} %mul.1983), kind=kOutput, calls=%fused_computation.210 | convolution fusion | flops 2420281600 | bytes 27953760 | tf_op jit(solution)/shard_map/dot_general | solution.py:146
  344.8 9.4 %fusion.290 = (f32[300]{0:T(512)S(1)}, f32[300]{0:T(512)S(1)}, f32[3240,300]{0,1:T(8,128)}) fusion(f32[3240,300]{0,1:T(8,128)} %copy.31, bf16[3240,1200]{0,1:T(8,128)(2,1)} %copy-done.139, bf16[300,1200]{1,0:T(8,128)(2,1)S(1)} %copy-done.28), kind=kOutput, calls=%fused_computation.661 | convolution fusion | flops 2335715584 | bytes 16274400 | tf_op jit(solution)/shard_map/dot_general | solution.py:150
  365.7 39.2 %all-reduce.5 = (f32[300]{0:T(512)S(1)}, f32[300]{0:T(512)S(1)}) all-reduce(f32[300]{0:T(512)S(1)} %get-tuple-element.21, f32[300]{0:T(512)S(1)} %get-tuple-element.20), channel_id=1, replica_groups=mesh['dp'=8,'fsdp'=4] {'dp','fsdp'}, use_global_device_ids=true, to_apply=%region_9.10 | all-reduce | flops 600 | bytes 4800 | tf_op jit(solution)/shard_map/psum | solution.py:152
  405.1 17.5 %fusion.124 = (f32[300]{0:T(512)S(1)}, f32[300]{0:T(512)}, f32[300]{0:T(512)}, f32[300]{0:T(512)}, f32[300]{0:T(512)}, /*index=5*/f32[300]{0:T(512)}, f32[300]{0...) fusion(bf16[1,18,178,300]{3,2,1,0:T(8,128)(2,1)} %get-tuple-element.249, ...), kind=kLoop, calls=%fused_computation.380 | loop fusion | flops 62205300 | bytes 27244564 | tf_op jit(solution)/shard_map/reduce_sum | solution.py:60
  422.8 11.1 %fusion.127 = (f32[300]{0:T(512)S(1)}, f32[300]{0:T(512)}, f32[300]{0:T(512)}, f32[300]{0:T(512)}, f32[300]{0:T(512)}, /*index=5*/f32[300]{0:T(512)}, f32[300]{0:T(512)}, f32[300]{0:T(512)}, f32[300]{0:T(512)}) fusion(bf16[1,18,180,300]{3,2,1,0:T(8,128)(2,1)S(1)} %get-tuple-element.122, bf16[1,18,1,300]{3,2,1,0:T(2,128)(2,1)S(1)} %copy-done.69, ...), kind=kLoop, calls=%fused_computation.383 | loop fusion | flops 53457300 | bytes 19450800 | tf_op jit(solution)/shard_map/reduce_sum | solution.py:60
  434.1 13.7 %fusion.128 = (f32[300]{0:T(512)}, f32[300]{0:T(512)}, f32[300]{0:T(512)}, f32[300]{0:T(512)}, f32[300]{0:T(512)}, /*index=5*/f32[300]{0:T(512)}, f32[300]{0:T(512)}, f32[300]{0:T(512)}, f32[300]{0:T(512)}) fusion(bf16[1,18,180,300]{3,2,1,0:T(8,128)(2,1)S(1)} %get-tuple-element.122, bf16[1,18,2,300]{3,2,1,0:T(2,128)(2,1)} %copy-done.86, ...), kind=kLoop, calls=%fused_computation.384 | loop fusion | flops 53457300 | bytes 19450800 | tf_op jit(solution)/shard_map/reduce_sum | solution.py:60
  447.9 13.1 %fusion.123 = (f32[300]{0:T(512)}, f32[300]{0:T(512)}, f32[300]{0:T(512)}, f32[300]{0:T(512)}, f32[300]{0:T(512)}, /*index=5*/f32[300]{0:T(512)}, f32[300]{0:T(512)}, f32[300]{0:T(512)}, f32[300]{0:T(512)}) fusion(bf16[1,18,180,300]{3,2,1,0:T(8,128)(2,1)S(1)} %get-tuple-element.122, bf16[1,18,177,300]{3,2,1,0:T(8,128)(2,1)} %get-tuple-element.237, ...), kind=kLoop, calls=%fused_computation.379 | loop fusion | flops 53457300 | bytes 19450800 | tf_op jit(solution)/shard_map/reduce_sum | solution.py:60
  461.1 9.5 %fusion.101 = (f32[300]{0:T(512)}, f32[300]{0:T(512)}, f32[300]{0:T(512)}, f32[300]{0:T(512)}, f32[300]{0:T(512)}, /*index=5*/f32[300]{0:T(512)}) fusion(bf16[1,18,180,300]{3,2,1,0:T(8,128)(2,1)S(1)} %get-tuple-element.122, bf16[1,18,180,300]{3,2,1,0:T(8,128)(2,1)S(1)} %copy-done.1, bf16[1,3,180,300]{3,2,1,0:T(8,128)(2,1)S(1)} %get-tuple-element.303, ...), kind=kLoop, calls=%fused_computation.357 | loop fusion | flops 39850200 | bytes 9986400 | tf_op jit(solution)/shard_map/reduce_sum | solution.py:60
  470.7 15.1 %fusion.129 = (f32[300]{0:T(512)}, f32[300]{0:T(512)}, f32[300]{0:T(512)}, f32[300]{0:T(512)}, f32[300]{0:T(512)}, /*index=5*/f32[300]{0:T(512)}, f32[300]{0:T(512)}) fusion(bf16[1,18,180,300]{3,2,1,0:T(8,128)(2,1)S(1)} %get-tuple-element.122, bf16[1,3,180,300]{3,2,1,0:T(8,128)(2,1)S(1)} %get-tuple-element.302, bf16[1,18,180,300]{3,2,1,0:T(8,128)(2,1)S(1)} %copy-done.1, ...), kind=kLoop, calls=%fused_computation.385 | loop fusion | flops 42765900 | bytes 9987600 | tf_op jit(solution)/shard_map/reduce_sum | solution.py:60
  492.5 8.0 %convolution_add_fusion.1 = f32[3240,300]{0,1:T(8,128)} fusion(bf16[3240,1200]{0,1:T(8,128)(2,1)} %get-tuple-element.297, bf16[1200,300]{1,0:T(8,128)(2,1)S(1)} %copy-done.27, f32[300]{0:T(512)S(1)} %copy-done.133), kind=kOutput, calls=%fused_computation.262 | convolution fusion | flops 2333772032 | bytes 12385200 | tf_op jit(solution)/shard_map/dot_general | solution.py:126
  538.7 7.1 stack.199
  545.8 43.7 %all-reduce.4 = (f32[300,49]{0,1:T(8,128)}, f32[1200]{0:T(1024)S(1)}, f32[300]{0:T(512)S(1)}) all-reduce(f32[300,49]{0,1:T(8,128)} %stack.199, f32[1200]{0:T(1024)S(1)} %copy-done.118, f32[300]{0:T(512)} %get-tuple-element.295), channel_id=1, replica_groups=mesh['dp'=8,'fsdp'=4] {'dp','fsdp'}, use_global_device_ids=true, to_apply=%region_59.60 | all-reduce | flops 16200 | bytes 129600 | tf_op jit(solution)/shard_map/psum | solution.py:166
  598.4 10.2 %fusion.196 = (bf16[1,18,179,300]{3,2,1,0:T(8,128)(2,1)}, bf16[1,18,179,300]{3,2,1,0:T(8,128)(2,1)}, bf16[1,18,179,300]{3,2,1,0:T(8,128)(2,1)}, bf16[1,18,179,30...) fusion(bf16[1,3,180,300]{3,2,1,0:T(8,128)(2,1)S(1)} %broadcast_, ...), kind=kLoop, calls=%fused_computation.462 | loop fusion | flops 5799600 | bytes 19043568 | tf_op jit(solution)/shard_map/concatenate | solution.py:73
  608.6 10.0 %fusion.195 = (bf16[1,18,178,300]{3,2,1,0:T(8,128)(2,1)}, bf16[1,18,178,300]{3,2,1,0:T(8,128)(2,1)}, bf16[1,18,178,300]{3,2,1,0:T(8,128)(2,1)}, bf16[1,18,178,30...) fusion(bf16[1,3,180,300]{3,2,1,0:T(8,128)(2,1)S(1)} %broadcast_, ...), kind=kLoop, calls=%fused_computation.461 | loop fusion | flops 5767200 | bytes 18967968 | tf_op jit(solution)/shard_map/concatenate | solution.py:73
  618.6 6.9 fusion.194
  631.5 7.0 fusion.176
  638.6 7.0 fusion.175
  646.4 72.5 %fusion.220 = bf16[1,1,18,180,300]{4,3,2,1,0:T(8,128)(2,1)} fusion(f32[18,180]{1,0:T(8,128)S(1)} %get-tuple-element.126, bf16[1,18,180,300]{3,2,1,0:T(8,128)(2,1)S(1)} %get-tuple-element.122, bf16[1,3,180,300]{3,2,1,0:T(8,128)(2,1)S(1)} %broadcast_select_fusion.2, bf16[1,18,3,300]{3,2,1,0:T(4,128)(2,1)S(1)} %get-tuple-element.174, ...), kind=kLoop, calls=%fused_computation.531 | loop fusion | flops 289656000 | bytes 84376560 | tf_op jit(solution)/shard_map/broadcast_in_dim | solution.py:173
  718.9 14.2 %all-reduce.11.cloned.1.call-done = (f32[300,1200]{1,0:T(8,128)}, f32[1200,300]{1,0:T(8,128)}) async-done(((f32[300,1200]{1,0:T(8,128)}, f32[1200,300]{1,0:T(8,128)}), (f32[300,1200]{1,0:T(8,128)}, f32[1200,300]{1,0:T(8,128)})) %all-reduce.11.cloned.1.call-update) | async-done | bytes 2880016 | tf_op jit(solution)/shard_map/psum | solution.py:166
  (414 shorter events, 139.7 us)
Async XLA Ops:
  7.2 725.9 %all-reduce.11.cloned.1.call-start = ((), (), s32[]{:S(2)}) async-start(), calls=%async_computation | async-start | bytes 6799360 | tf_op jit(solution)/shard_map/psum | solution.py:166
  10.3 112.1 %copy-start = (bf16[1,18,180,300]{3,2,1,0:T(8,128)(2,1)}, bf16[1,18,180,300]{3,2,1,0:T(8,128)(2,1)S(1)}, u32[]{:S(2)}) copy-start(bf16[1,18,180,300]{3,2,1,0:T(8,128)(2,1)S(1)} %bitcast_multiply_fusion) | copy-start | bytes 5832004
  11.4 56.7 %collective-permute-start = (bf16[1,3,180,300]{3,2,1,0:T(8,128)(2,1)}, bf16[1,3,180,300]{3,2,1,0:T(8,128)(2,1)}, u32[]{:S(2)}, u32[]{:S(2)}) collective-permute-start(bf16[1,3,180,300]{3,2,1,0:T(8,128)(2,1)} %get-tuple-element.288), channel_id=1, source_target_pairs={{0,4},{4,8},{8,12},{12,16},{16,20},{20,24},{24,28},{1,5},{5,9},{9,... | collective-permute-start | bytes 972008 | tf_op jit(solution)/shard_map/ppermute | solution.py:20
  17.0 51.1 %collective-permute-start.1 = (bf16[1,3,180,300]{3,2,1,0:T(8,128)(2,1)}, bf16[1,3,180,300]{3,2,1,0:T(8,128)(2,1)}, u32[]{:S(2)}, u32[]{:S(2)}) collective-permute-start(bf16[1,3,180,300]{3,2,1,0:T(8,128)(2,1)} %get-tuple-element.289), channel_id=1, source_target_pairs={{4,0},{8,4},{12,8},{16,12},{20,16},{24,20},{28,24},{5,1},{9,5},{13... | collective-permute-start | bytes 972008 | tf_op jit(solution)/shard_map/ppermute | solution.py:21
  64.1 58.3 %copy-start.87 = (f32[300]{0:T(512)}, f32[300]{0:T(512)S(1)}, u32[]{:S(2)}) copy-start(f32[300]{0:T(512)S(1)} %get-tuple-element.98) | copy-start | bytes 3604
  64.1 58.3 %copy-start.89 = (f32[300]{0:T(512)}, f32[300]{0:T(512)S(1)}, u32[]{:S(2)}) copy-start(f32[300]{0:T(512)S(1)} %get-tuple-element.99) | copy-start | bytes 3604
  122.1 78.5 %copy-start.48 = (bf16[1,18,2,300]{3,2,1,0:T(2,128)(2,1)}, bf16[1,18,2,300]{3,2,1,0:T(2,128)(2,1)S(1)}, u32[]{:S(2)}) copy-start(bf16[1,18,2,300]{3,2,1,0:T(2,128)(2,1)S(1)} %get-tuple-element.239) | copy-start | bytes 64804
  122.1 78.5 %copy-start.49 = (bf16[1,18,2,300]{3,2,1,0:T(2,128)(2,1)}, bf16[1,18,2,300]{3,2,1,0:T(2,128)(2,1)S(1)}, u32[]{:S(2)}) copy-start(bf16[1,18,2,300]{3,2,1,0:T(2,128)(2,1)S(1)} %get-tuple-element.240) | copy-start | bytes 64804
  122.1 78.5 %copy-start.50 = (bf16[1,18,2,300]{3,2,1,0:T(2,128)(2,1)}, bf16[1,18,2,300]{3,2,1,0:T(2,128)(2,1)S(1)}, u32[]{:S(2)}) copy-start(bf16[1,18,2,300]{3,2,1,0:T(2,128)(2,1)S(1)} %get-tuple-element.243) | copy-start | bytes 64804
  122.2 78.5 %copy-start.66 = (bf16[1,18,2,300]{3,2,1,0:T(2,128)(2,1)}, bf16[1,18,2,300]{3,2,1,0:T(2,128)(2,1)S(1)}, u32[]{:S(2)}) copy-start(bf16[1,18,2,300]{3,2,1,0:T(2,128)(2,1)S(1)} %get-tuple-element.291) | copy-start | bytes 64804
  122.2 78.5 %copy-start.72 = (bf16[1,18,2,300]{3,2,1,0:T(2,128)(2,1)}, bf16[1,18,2,300]{3,2,1,0:T(2,128)(2,1)S(1)}, u32[]{:S(2)}) copy-start(bf16[1,18,2,300]{3,2,1,0:T(2,128)(2,1)S(1)} %get-tuple-element.241) | copy-start | bytes 64804
  122.2 78.5 %copy-start.74 = (bf16[1,18,2,300]{3,2,1,0:T(2,128)(2,1)}, bf16[1,18,2,300]{3,2,1,0:T(2,128)(2,1)S(1)}, u32[]{:S(2)}) copy-start(bf16[1,18,2,300]{3,2,1,0:T(2,128)(2,1)S(1)} %get-tuple-element.242) | copy-start | bytes 64804
  122.2 78.5 %copy-start.86 = (bf16[1,18,2,300]{3,2,1,0:T(2,128)(2,1)}, bf16[1,18,2,300]{3,2,1,0:T(2,128)(2,1)S(1)}, u32[]{:S(2)}) copy-start(bf16[1,18,2,300]{3,2,1,0:T(2,128)(2,1)S(1)} %get-tuple-element.244) | copy-start | bytes 64804
  122.4 78.4 %copy-start.51 = (bf16[1,18,1,300]{3,2,1,0:T(2,128)(2,1)}, bf16[1,18,1,300]{3,2,1,0:T(2,128)(2,1)S(1)}, u32[]{:S(2)}) copy-start(bf16[1,18,1,300]{3,2,1,0:T(2,128)(2,1)S(1)} %get-tuple-element.251) | copy-start | bytes 32404
  122.4 78.4 %copy-start.52 = (bf16[1,18,1,300]{3,2,1,0:T(2,128)(2,1)}, bf16[1,18,1,300]{3,2,1,0:T(2,128)(2,1)S(1)}, u32[]{:S(2)}) copy-start(bf16[1,18,1,300]{3,2,1,0:T(2,128)(2,1)S(1)} %get-tuple-element.252) | copy-start | bytes 32404
  122.4 78.4 %copy-start.53 = (bf16[1,18,1,300]{3,2,1,0:T(2,128)(2,1)}, bf16[1,18,1,300]{3,2,1,0:T(2,128)(2,1)S(1)}, u32[]{:S(2)}) copy-start(bf16[1,18,1,300]{3,2,1,0:T(2,128)(2,1)S(1)} %get-tuple-element.293) | copy-start | bytes 32404
  122.4 78.4 %copy-start.56 = (bf16[1,18,1,300]{3,2,1,0:T(2,128)(2,1)}, bf16[1,18,1,300]{3,2,1,0:T(2,128)(2,1)S(1)}, u32[]{:S(2)}) copy-start(bf16[1,18,1,300]{3,2,1,0:T(2,128)(2,1)S(1)} %get-tuple-element.255) | copy-start | bytes 32404
  122.4 78.4 %copy-start.68 = (bf16[1,18,1,300]{3,2,1,0:T(2,128)(2,1)}, bf16[1,18,1,300]{3,2,1,0:T(2,128)(2,1)S(1)}, u32[]{:S(2)}) copy-start(bf16[1,18,1,300]{3,2,1,0:T(2,128)(2,1)S(1)} %get-tuple-element.256) | copy-start | bytes 32404
  122.4 78.4 %copy-start.76 = (bf16[1,18,1,300]{3,2,1,0:T(2,128)(2,1)}, bf16[1,18,1,300]{3,2,1,0:T(2,128)(2,1)S(1)}, u32[]{:S(2)}) copy-start(bf16[1,18,1,300]{3,2,1,0:T(2,128)(2,1)S(1)} %get-tuple-element.253) | copy-start | bytes 32404
  122.4 78.4 %copy-start.78 = (bf16[1,18,1,300]{3,2,1,0:T(2,128)(2,1)}, bf16[1,18,1,300]{3,2,1,0:T(2,128)(2,1)S(1)}, u32[]{:S(2)}) copy-start(bf16[1,18,1,300]{3,2,1,0:T(2,128)(2,1)S(1)} %get-tuple-element.254) | copy-start | bytes 32404
  512.4 26.1 %copy-start.108 = (f32[300]{0:T(512)S(1)}, f32[300]{0:T(512)}, u32[]{:S(2)}) copy-start(f32[300]{0:T(512)} %get-tuple-element.12) | copy-start | bytes 3604
  512.4 26.1 %copy-start.106 = (f32[300]{0:T(512)S(1)}, f32[300]{0:T(512)}, u32[]{:S(2)}) copy-start(f32[300]{0:T(512)} %get-tuple-element.13) | copy-start | bytes 3604
  512.4 26.1 %copy-start.105 = (f32[300]{0:T(512)S(1)}, f32[300]{0:T(512)}, u32[]{:S(2)}) copy-start(f32[300]{0:T(512)} %get-tuple-element.9) | copy-start | bytes 3604
  512.4 26.1 %copy-start.96 = (f32[300]{0:T(512)S(1)}, f32[300]{0:T(512)}, u32[]{:S(2)}) copy-start(f32[300]{0:T(512)} %get-tuple-element.43) | copy-start | bytes 3604
  512.5 26.1 %copy-start.95 = (f32[300]{0:T(512)S(1)}, f32[300]{0:T(512)}, u32[]{:S(2)}) copy-start(f32[300]{0:T(512)} %get-tuple-element.44) | copy-start | bytes 3604
  512.5 26.1 %copy-start.94 = (f32[300]{0:T(512)S(1)}, f32[300]{0:T(512)}, u32[]{:S(2)}) copy-start(f32[300]{0:T(512)} %get-tuple-element.45) | copy-start | bytes 3604
  512.5 26.1 %copy-start.93 = (f32[300]{0:T(512)S(1)}, f32[300]{0:T(512)}, u32[]{:S(2)}) copy-start(f32[300]{0:T(512)} %get-tuple-element.46) | copy-start | bytes 3604
  512.5 26.2 %copy-start.92 = (f32[300]{0:T(512)S(1)}, f32[300]{0:T(512)}, u32[]{:S(2)}) copy-start(f32[300]{0:T(512)} %get-tuple-element.47) | copy-start | bytes 3604
  512.5 33.3 %copy-start.118 = (f32[1200]{0:T(1024)S(1)}, f32[1200]{0:T(1024)}, u32[]{:S(2)}) copy-start(f32[1200]{0:T(1024)} %get-tuple-element.300) | copy-start | bytes 14404
  512.5 77.6 %copy-start.45 = (bf16[1,3,180,300]{3,2,1,0:T(8,128)(2,1)S(1)}, bf16[1,3,180,300]{3,2,1,0:T(8,128)(2,1)}, u32[]{:S(2)}) copy-start(bf16[1,3,180,300]{3,2,1,0:T(8,128)(2,1)} %get-tuple-element.275) | copy-start | bytes 972004
  512.5 84.7 %collective-permute-start.2 = (bf16[1,3,180,300]{3,2,1,0:T(8,128)(2,1)S(1)}, bf16[1,3,180,300]{3,2,1,0:T(8,128)(2,1)}, u32[]{:S(2)}, u32[]{:S(2)}) collective-permute-start(bf16[1,3,180,300]{3,2,1,0:T(8,128)(2,1)S(1)} %copy-done.46), channel_id=1, source_target_pairs={{4,0},{8,4},{12,8},{16,12},{20,16},{24,20},{28,24},{5,1},{9,5},{13... | collective-permute-start | bytes 972008 | tf_op jit(solution)/shard_map/ppermute | solution.py:21
  590.1 35.7 %collective-permute-start.3 = (bf16[1,3,180,300]{3,2,1,0:T(8,128)(2,1)S(1)}, bf16[1,3,180,300]{3,2,1,0:T(8,128)(2,1)}, u32[]{:S(2)}, u32[]{:S(2)}) collective-permute-start(bf16[1,3,180,300]{3,2,1,0:T(8,128)(2,1)S(1)} %copy-done.45), channel_id=1, source_target_pairs={{0,4},{4,8},{8,12},{12,16},{16,20},{20,24},{24,28},{1,5},{5,9},{9,... | collective-permute-start | bytes 972008 | tf_op jit(solution)/shard_map/ppermute | solution.py:20
  (117 other events, 1471.0 us)
Sparse Core Ops, SparseCore 0:
  595.1 137.8 all-reduce.10
where the time goes:
time: 750 us; the launch traced here: 744 us
  other arithmetic  353 us (47%)
  blocking collectives  196 us (26%)
  local copies, waits for them, and re-layouts  87.9 us (12%)
  matrix products  60.6 us (8%)
  between operations  18.7 us (2%)
  waiting for transfers between devices  14.2 us (2%)
  starting transfers between devices  13.3 us (2%)
    concatenate x24, other arithmetic, cut_rims(): return jnp.concatenate([top, padded[:, span:-span], bottom], axis=1)  100 us
    reduce_sum x6, other arithmetic, kernel_terms(): columns.append(jnp.sum(shifted * gfloat, axis=(0, 1, 2)))  80 us
    reduce_sum x1, other arithmetic, local(): jnp.sum(conv_out * ocean, axis=(0, 1, 2))  78 us
    broadcast_in_dim x1, other arithmetic, local(): grad_features[None]  72.5 us
    psum x1, blocking collectives, local(): lax.psum((local_grads[0], local_grads[1], local_grads[2], local_grads[3],...  43.7 us
    psum x1, blocking collectives, local(): lax.psum((jnp.sum(conv_out * ocean, axis=(0, 1, 2)), local_count), ('dp',...  41.7 us
    psum x1, blocking collectives, local(): lax.psum(jnp.sum(ocean * centered * centered, axis=(0, 1, 2)), ('dp', 'fs...  41.2 us
    psum x1, blocking collectives, local(): lax.psum((jnp.sum(gz_rows * normed_rows, axis=0), jnp.sum(gz_rows, axis=0...  39.2 us
  transfers between devices with their start and end apart: 5, of which 1 were waited for; matrix products, arithmetic and copies ran while one was open for 23% of the time, Pallas kernels for 0%

commit v1 on v0

v1 whole, which is shorter than its diff:
```python
import functools

import jax
import jax.numpy as jnp
import numpy as np
from jax import lax
from jax.experimental import pallas as pl
from jax.experimental.pallas import tpu as pltpu
from jax.sharding import PartitionSpec as P

KW = 7
SPAN = KW // 2
TILES = 8
EPSILON = 1e-05

LANES = 128
HALF = 64
FINE = 12
PAD = 16
PASSES = (KW + 1) // 2
TAPS = KW * KW
BASE = 8

F32 = jnp.float32
BF16 = jnp.bfloat16
LIMIT = 60 * 2**20
WHOLE = pl.BlockSpec(memory_space=pltpu.VMEM)
HBM = pl.BlockSpec(memory_space=pl.ANY)


def round_up(value, step):
    return -(-value // step) * step


def call(kernel, outs, operands, in_specs, scratch=(), flops=0, moved=0, grid=None, out_specs=None, name=None):
    extra = {} if grid is None else {"grid": grid}
    return pl.pallas_call(
        kernel,
        out_shape=[jax.ShapeDtypeStruct(shape, dtype) for shape, dtype in outs],
        in_specs=in_specs,
        out_specs=[WHOLE] * len(outs) if out_specs is None else out_specs,
        scratch_shapes=list(scratch),
        compiler_params=pltpu.CompilerParams(vmem_limit_bytes=LIMIT),
        cost_estimate=pl.CostEstimate(flops=flops, bytes_accessed=moved, transcendentals=0),
        name=name,
        **extra,
    )(*operands)


def low_half(rows):
    return lax.broadcasted_iota(jnp.int32, (rows, LANES), 1) < HALF


def swap(value):
    return pltpu.roll(value, HALF, 1)


def tiles_of(channels):
    return [(t, min(LANES, channels - t * LANES)) for t in range(-(-channels // LANES))]


def mask_column(land_t, row):
    lane = lax.broadcasted_iota(jnp.int32, land_t.shape, 1)
    return jnp.sum(jnp.where(lane == row, land_t, 0.0), axis=1, keepdims=True)


def stage_row(stage, values, width):
    lanes = values.shape[1]
    stage[0, BASE : BASE + width, :lanes] = values
    stage[0, BASE - SPAN : BASE, :lanes] = values[width - SPAN :]
    stage[0, BASE + width : BASE + width + SPAN, :lanes] = values[:SPAN]
    stage[1] = swap(stage[0])


def plane(stage, which, start):
    return stage[which, pl.ds(start, PAD, stride=FINE), :]


def place_row(paired, stage, tile, blocks, pair, side):
    low = low_half(PAD)
    lanes = pl.ds(side * LANES, LANES)
    for k in range((FINE + 2 * SPAN) // 2):
        start = BASE - SPAN + 2 * k
        paired[2 * tile, pair, k, :, lanes] = jnp.where(
            low, plane(stage, 0, start), plane(stage, 1, start + 1)
        ).astype(BF16)
        if 2 * tile + 1 < blocks:
            paired[2 * tile + 1, pair, k, :, lanes] = jnp.where(
                low, plane(stage, 1, start), plane(stage, 0, start + 1)
            ).astype(BF16)


def place_natural(paired, stage, source, channels, width, blocks, pair, side, factor=None):
    for t, lanes in tiles_of(channels):
        values = source(t * LANES, t * LANES + lanes).astype(F32)
        if factor is not None:
            values = values * factor
        buffer = stage.at[side, t]
        stage_row(buffer, values, width)
        place_row(paired, buffer, t, blocks, pair, side)


def place_rims(paired, stage, top, bottom, channels, width, blocks, height):
    for index in range(SPAN):
        for source, row in ((top, index), (bottom, SPAN + height + index)):
            place_natural(
                paired,
                stage,
                lambda a, b, source=source, index=index: source[index, :, a:b],
                channels,
                width,
                blocks,
                row // 2,
                row % 2,
            )


def build_weights(weights, taps, block, flip):
    lane = lax.broadcasted_iota(jnp.int32, (HALF, LANES), 1)
    sub = lax.broadcasted_iota(jnp.int32, (HALF, LANES), 0)
    diagonal = lax.rem(lane, HALF) == sub
    low = low_half(1)
    zero = jnp.zeros((1, LANES), F32)

    def tap_row(a, b):
        if not (0 <= a < KW and 0 <= b < KW):
            return zero
        index = (KW - 1 - a) * KW + KW - 1 - b if flip else a * KW + b
        return taps[block, index : index + 1, :]

    for m in range(PASSES):
        for s in range(PASSES):
            for place in range(4):
                pr, pj = divmod(place, 2)
                for qr in range(2):
                    a, b = 2 * m + pr - qr, 2 * s + pj
                    row = jnp.where(low, tap_row(a, b), tap_row(a, b - 1))
                    weights[
                        (m * PASSES + s) * 4 * HALF + place * HALF : (m * PASSES + s) * 4 * HALF + (place + 1) * HALF,
                        qr * LANES : (qr + 1) * LANES,
                    ] = jnp.where(diagonal, row, 0.0).astype(BF16)


def pass_rows(paired, block, m, s, pairs):
    piece = paired[block, m : m + pairs, s : s + FINE // 2]
    return piece.reshape(pairs * (FINE // 2) * PAD, 4 * HALF)


def convolve_block(paired, weights, block, pairs):
    rows = jnp.concatenate(
        [pass_rows(paired, block, m, s, pairs) for m in range(PASSES) for s in range(PASSES)], axis=1
    )
    return jnp.dot(rows, weights[...], preferred_element_type=F32)


def split_blocks(lower, upper, start, side):
    low = low_half(PAD)
    rows, lanes = pl.ds(start, PAD), pl.ds(side * LANES, LANES)
    first = lower[rows, lanes]
    if upper is None:
        return first, swap(first)
    second = upper[rows, lanes]
    return jnp.where(low, first, swap(second)), jnp.where(low, swap(first), second)


def prepare_kernel(feats, cot, land_t, paired, gbranch, mask, stage, plain):
    height, width, channels = feats.shape
    blocks = paired.shape[0]
    stage[...] = jnp.zeros_like(stage)
    plain[...] = jnp.zeros_like(plain)

    def one(row, pair, side):
        factor = mask_column(land_t[...], row)
        place_natural(
            paired, stage, lambda a, b: feats[row, :, a:b], channels, width, blocks, pair, side, factor
        )
        rows = pl.ds(BASE, width)
        plain[side, 0, rows, :] = jnp.broadcast_to(factor, (width, LANES))
        for t, lanes in tiles_of(channels):
            plain[side, 1 + t, rows, :lanes] = cot[row, :, t * LANES : t * LANES + lanes].astype(F32) * factor
        for r in range(FINE):
            mask[row, r] = plain[side, 0, pl.ds(BASE + r, PAD, stride=FINE), :]
            for t, _ in tiles_of(channels):
                gbranch[row, r, :, t * LANES : (t + 1) * LANES] = plain[
                    side, 1 + t, pl.ds(BASE + r, PAD, stride=FINE), :
                ].astype(BF16)

    one(0, SPAN // 2, SPAN % 2)

    def step(pair, _):
        one(2 * pair - SPAN, pair, 0)
        one(2 * pair + 1 - SPAN, pair, 1)
        return 0

    lax.fori_loop(SPAN // 2 + 1, (SPAN + height) // 2, step, 0)
    one(height - 1, (SPAN + height - 1) // 2, (SPAN + height - 1) % 2)


def forward_kernel(channels, paired_hbm, top, bottom, taps, mask, conv, stats, paired, weights, accs, stage, sem):
    height = conv.shape[0]
    blocks, pairs = paired.shape[0], height // 2
    width = top.shape[1]
    copy = pltpu.make_async_copy(paired_hbm, paired, sem)
    copy.start()
    stage[...] = jnp.zeros_like(stage)
    copy.wait()
    place_rims(paired, stage, top, bottom, channels, width, blocks, height)
    conv[...] = jnp.zeros_like(conv)
    for t, _ in tiles_of(channels):
        lanes = pl.ds(t * LANES, LANES)
        has_upper = 2 * t + 1 < blocks
        for half in range(1 + has_upper):
            build_weights(weights, taps, 2 * t + half, False)
            accs[half] = convolve_block(paired, weights, 2 * t + half, pairs)

        def spread(h, sums, t=t, lanes=lanes, has_upper=has_upper):
            total, count = sums
            for k in range(FINE // 2):
                for side in range(2):
                    even, odd = split_blocks(
                        accs.at[0], accs.at[1] if has_upper else None, (h * (FINE // 2) + k) * PAD, side
                    )
                    row = 2 * h + side
                    conv[row, 2 * k, :, lanes] = even
                    conv[row, 2 * k + 1, :, lanes] = odd
                    first, second = mask[row, 2 * k], mask[row, 2 * k + 1]
                    total = total + first * even + second * odd
                    count = count + first + second
            return total, count

        zero = jnp.zeros((PAD, LANES), F32)
        total, count = lax.fori_loop(0, pairs, spread, (zero, zero))
        total = jnp.sum(total, axis=0, keepdims=True)
        count = jnp.sum(count, axis=0, keepdims=True)
        mean = total / jnp.maximum(count, 1.0)

        def deviate(row, sums, lanes=lanes, mean=mean):
            for r in range(FINE):
                away = conv[row, r, :, lanes] - mean
                sums = sums + mask[row, r] * (away * away)
            return sums

        spread_sum = lax.fori_loop(0, height, deviate, zero)
        stats[0:1, lanes] = mean
        stats[1:2, lanes] = jnp.sum(spread_sum, axis=0, keepdims=True)


def pointwise_kernel(
    channels, real_units, conv, gbranch, feats, land_t, mask, vec, w_in, w_out, w_in_t, w_out_t,
    output, act_out, ghid_out, gz_out, z_out, sums, stage,
):
    rows, width = feats.shape[0], feats.shape[1]
    padded = conv.shape[-1]
    cells = rows * FINE * PAD
    hidden_units = act_out.shape[1]
    step = pl.program_id(0)

    @pl.when(step == 0)
    def _():
        sums[...] = jnp.zeros_like(sums)

    one_lane = lax.broadcasted_iota(jnp.int32, (1, padded), 1) == channels
    mean, inverse, gain, shift = (vec[i : i + 1, :] for i in range(4))
    normed = (conv[...].reshape(cells, padded) - mean) * inverse
    zvals = jnp.where(one_lane, 1.0, gain * normed + shift).astype(BF16)
    z_out[...] = zvals
    upstream = gbranch[...].reshape(cells, padded)
    branch = jnp.zeros((cells, padded), F32)
    gz = jnp.zeros((cells, padded), F32)
    chunk = 2 * LANES
    c0 = 0.7978845608028654
    c1 = 0.044715 * c0
    for start in range(0, hidden_units, chunk):
        span = pl.ds(start, chunk)
        hidden = jnp.dot(zvals, w_in[:, span], preferred_element_type=F32)
        gact = jnp.dot(upstream, w_out_t[:, span], preferred_element_type=F32)
        square = hidden * hidden
        bent = jnp.tanh(hidden * (c0 + c1 * square))
        half = 0.5 * hidden
        act = half + half * bent
        slope = (0.5 + 0.5 * bent) + half * (1.0 - bent * bent) * (c0 + (3.0 * c1) * square)
        ghid = (gact * slope).astype(BF16)
        act = act.astype(BF16)
        if start + chunk > real_units:
            lane = lax.broadcasted_iota(jnp.int32, (1, chunk), 1)
            act = jnp.where(lane == real_units - start, jnp.ones((), BF16), act)
        act_out[:, span] = act
        ghid_out[:, span] = ghid
        branch = branch + jnp.dot(act, w_out[span, :], preferred_element_type=F32)
        gz = gz + jnp.dot(ghid, w_in_t[span, :], preferred_element_type=F32)
    gz_out[...] = gz.reshape(gz_out.shape)
    sums[0:1, :] += jnp.sum(gz * normed, axis=0, keepdims=True)
    sums[1:2, :] += jnp.sum(gz, axis=0, keepdims=True)
    for row in range(rows):
        factor = mask_column(land_t[...], step * rows + row)
        for t, lanes in tiles_of(channels):
            for r in range(FINE):
                start = (row * FINE + r) * PAD
                stage[row, t, pl.ds(r, PAD, stride=FINE), :] = branch[start : start + PAD, t * LANES : (t + 1) * LANES]
            piece = pl.ds(t * LANES, lanes)
            values = feats[row, :, piece].astype(F32) + stage[row, t, 0:width, :lanes]
            output[row, :, piece] = (values * factor).astype(BF16)


def weight_kernel(zvals, ghid, gbranch, act, grad_in, grad_out):
    @pl.when(pl.program_id(0) == 0)
    def _():
        grad_in[...] = jnp.zeros_like(grad_in)
        grad_out[...] = jnp.zeros_like(grad_out)

    over_rows = (((0,), (0,)), ((), ()))
    rows = grad_in.shape[0]
    grad_in[...] += lax.dot_general(zvals[:, :rows], ghid[...], over_rows, preferred_element_type=F32)
    grad_out[...] += lax.dot_general(gbranch[:, :rows], act[...], over_rows, preferred_element_type=F32)


def gradient_kernel(
    channels, gz, conv, mask, vec, paired_hbm, top, bottom, select, gconv, grad_taps, paired, own, stage, sem
):
    height = gz.shape[0]
    blocks, pairs = paired.shape[0], height // 2
    width = top.shape[1]
    copy = pltpu.make_async_copy(paired_hbm, paired, sem)
    copy.start()
    stage[...] = jnp.zeros_like(stage)
    low = low_half(PAD)

    def arrange(h, _):
        for t, _unused in tiles_of(channels):
            lanes = pl.ds(t * LANES, LANES)
            mean, inverse, scaled, bias, slope = (vec[i : i + 1, lanes] for i in range(5))
            for k in range(FINE // 2):
                rows = pl.ds((h * (FINE // 2) + k) * PAD, PAD)
                for side in range(2):
                    both = []
                    for r in (2 * k, 2 * k + 1):
                        row = 2 * h + side
                        normed = (conv[row, r, :, lanes] - mean) * inverse
                        value = scaled * gz[row, r, :, lanes] - mask[row, r] * (bias + normed * slope)
                        gconv[row, r, :, lanes] = value.astype(BF16)
                        both.append(value)
                    out_lanes = pl.ds(side * LANES, LANES)
                    own[2 * t, rows, out_lanes] = jnp.where(low, both[0], swap(both[1])).astype(BF16)
                    if 2 * t + 1 < blocks:
                        own[2 * t + 1, rows, out_lanes] = jnp.where(low, swap(both[0]), both[1]).astype(BF16)
        return 0

    lax.fori_loop(0, pairs, arrange, 0)
    copy.wait()
    place_rims(paired, stage, top, bottom, channels, width, blocks, height)
    lane = lax.broadcasted_iota(jnp.int32, (HALF, 2 * LANES), 1)
    sub = lax.broadcasted_iota(jnp.int32, (HALF, 2 * LANES), 0)
    diagonal = lax.rem(lane, HALF) == sub

    def one_block(block, _):
        turned = own[block].T
        found = []
        for m in range(PASSES):
            for s in range(PASSES):
                product = jnp.dot(turned, pass_rows(paired, block, m, s, pairs), preferred_element_type=F32)
                for q in range(4):
                    part = product[q * HALF : (q + 1) * HALF]
                    found.append(jnp.sum(jnp.where(diagonal, part, 0.0), axis=0, keepdims=True))
        found = jnp.concatenate(found, axis=0)
        total = None
        for place in range(4):
            group = jnp.dot(
                select[place], found, preferred_element_type=F32, precision=lax.Precision.HIGHEST
            )
            group = group[:, (place // 2) * LANES : (place // 2 + 1) * LANES]
            if place % 2:
                group = swap(group)
            total = group if total is None else total + group
        grad_taps[block] = total
        return 0

    lax.fori_loop(0, blocks, one_block, 0)


def backward_kernel(channels, gconv, top, bottom, taps, mask, cot, land_t, result, paired, weights, accs, stage):
    height, width = cot.shape[0], cot.shape[1]
    blocks, pairs = paired.shape[0], height // 2
    real = width // FINE
    low = low_half(PAD)

    def planes(source, row, lanes):
        out = []
        for r in range(-SPAN, FINE + SPAN):
            value = source[row, r % FINE, :, lanes].astype(F32)
            if r < 0:
                value = jnp.concatenate([value[real - 1 : real], value[: PAD - 1]], axis=0)
            elif r >= FINE:
                value = jnp.concatenate([value[1:real], value[:1], value[: PAD - real]], axis=0)
            out.append(value)
        return out

    def place(source, row, pair, side):
        out_lanes = pl.ds(side * LANES, LANES)
        for t, _unused in tiles_of(channels):
            values = planes(source, row, pl.ds(t * LANES, LANES))
            for k in range((FINE + 2 * SPAN) // 2):
                first, second = values[2 * k], values[2 * k + 1]
                paired[2 * t, pair, k, :, out_lanes] = jnp.where(low, first, swap(second)).astype(BF16)
                if 2 * t + 1 < blocks:
                    paired[2 * t + 1, pair, k, :, out_lanes] = jnp.where(low, swap(first), second).astype(BF16)

    for index in range(SPAN):
        place(top, index, index // 2, index % 2)
        place(bottom, index, (SPAN + height + index) // 2, (SPAN + height + index) % 2)
    place(gconv, 0, SPAN // 2, SPAN % 2)
    place(gconv, height - 1, (SPAN + height - 1) // 2, (SPAN + height - 1) % 2)

    def body(pair, _):
        place(gconv, 2 * pair - SPAN, pair, 0)
        place(gconv, 2 * pair + 1 - SPAN, pair, 1)
        return 0

    lax.fori_loop(SPAN // 2 + 1, (SPAN + height) // 2, body, 0)
    for t, count in tiles_of(channels):
        has_upper = 2 * t + 1 < blocks
        for half in range(1 + has_upper):
            build_weights(weights, taps, 2 * t + half, True)
            accs[half] = convolve_block(paired, weights, 2 * t + half, pairs)

        def spread(h, _, t=t, count=count, has_upper=has_upper):
            for side in range(2):
                row = 2 * h + side
                for k in range(FINE // 2):
                    even, odd = split_blocks(
                        accs.at[0], accs.at[1] if has_upper else None, (h * (FINE // 2) + k) * PAD, side
                    )
                    stage[side, pl.ds(2 * k, PAD, stride=FINE), :] = even
                    stage[side, pl.ds(2 * k + 1, PAD, stride=FINE), :] = odd
                factor = mask_column(land_t[...], row)
                piece = pl.ds(t * LANES, count)
                values = cot[row, :, piece].astype(F32) + stage[side, 0:width, :count]
                result[row, :, piece] = (values * factor).astype(BF16)
            return 0

        lax.fori_loop(0, pairs, spread, 0)


def partners(size, bit):
    return [(i, i ^ bit) for i in range(size)]


def bits(size):
    bit = 1
    while bit < size:
        yield bit
        bit *= 2


def butterfly(values, merge, axes=("fsdp", "dp")):
    for axis in axes:
        size = lax.axis_size(axis)
        for bit in bits(size):
            values = merge(values, lax.ppermute(values, axis, partners(size, bit)))
    return values


def merge_stats(mine, other):
    count = mine[2:3] + other[2:3]
    safe = jnp.maximum(count, 1.0)
    mean = (mine[0:1] * mine[2:3] + other[0:1] * other[2:3]) / safe
    away = mine[0:1] - other[0:1]
    spread = mine[1:2] + other[1:2] + away * away * (mine[2:3] * other[2:3] / safe)
    return jnp.concatenate([mean, spread, count], axis=0)


def rims(array):
    size = lax.axis_size("dp")
    down = [(i, i + 1) for i in range(size - 1) if (i + 1) % TILES]
    up = [(j, i) for i, j in down]
    return lax.ppermute(array[-SPAN:], "dp", down), lax.ppermute(array[:SPAN], "dp", up)


def tap_selectors(rows):
    out = np.zeros((4, rows, PASSES * PASSES * 4), np.float32)
    for m in range(PASSES):
        for s in range(PASSES):
            for q in range(4):
                for p in range(4):
                    a = 2 * m + p // 2 - q // 2
                    b = 2 * s + p % 2 - q % 2
                    if 0 <= a < KW and 0 <= b < KW:
                        out[p, a * KW + b, (m * PASSES + s) * 4 + q] = 1.0
    return out


def own_share(value):
    share = value.shape[0] // lax.axis_size("fsdp")
    return lax.dynamic_slice_in_dim(value, lax.axis_index("fsdp") * share, share, 0)


def gather(value):
    return lax.all_gather(value, "fsdp", axis=0, tiled=True)


def local(features, land_mask, cotangent, kernel, norm_gain, norm_shift, in_proj, in_bias, out_proj, out_bias):
    feats, cot = features[0, 0], cotangent[0, 0]
    height, width, channels = feats.shape
    hidden = in_proj.shape[1]
    padded = round_up(channels + 1, LANES)
    hidden_pad = round_up(hidden + 1, 2 * LANES)
    blocks = -(-channels // HALF)
    pairs = height // 2
    planes_in = (FINE + 2 * SPAN) // 2
    row_pairs = (height + 2 * SPAN) // 2
    cells = height * FINE * PAD
    block_rows = pairs * (FINE // 2) * PAD
    stage_rows = round_up(BASE + SPAN + FINE * PAD, 8)
    tile_count = len(tiles_of(channels))

    tile_index = lax.axis_index("dp") % TILES
    land = lax.dynamic_slice_in_dim(land_mask, tile_index * height, height, 0)
    land_t = land.T.astype(F32)
    low_mask = land.astype(BF16)[:, :, None]
    edge = jnp.concatenate([feats[:SPAN] * low_mask[:SPAN], feats[-SPAN:] * low_mask[-SPAN:]], axis=0)
    top, bottom = rims(edge)

    paired_shape = (blocks, row_pairs, planes_in, PAD, 4 * HALF)
    plane_shape = (height, FINE, PAD, padded)
    mask_shape = (height, FINE, PAD, LANES)
    stage = pltpu.VMEM((2, tile_count, 2, stage_rows, LANES), F32)
    paired, gbranch, mask = call(
        prepare_kernel,
        [(paired_shape, BF16), (plane_shape, BF16), (mask_shape, F32)],
        (feats, cot, land_t),
        [WHOLE] * 3,
        [stage, pltpu.VMEM((2, 1 + tile_count, stage_rows, LANES), F32)],
        moved=20 * 2**20,
        name="prepare",
    )

    taps_full = gather(kernel)
    taps = jnp.pad(taps_full.astype(F32), ((0, blocks * HALF - channels), (0, 0)))
    taps = jnp.swapaxes(taps.reshape(blocks, HALF, TAPS), 1, 2)
    taps = jnp.concatenate([taps, taps], axis=2)
    accs = pltpu.VMEM((2, block_rows, 4 * HALF), F32)
    weights = pltpu.VMEM((PASSES * PASSES * 4 * HALF, 4 * HALF), BF16)
    conv, stats = call(
        functools.partial(forward_kernel, channels),
        [(plane_shape, F32), ((8, padded), F32)],
        (paired, top, bottom, taps, mask),
        [HBM] + [WHOLE] * 4,
        [pltpu.VMEM(paired_shape, BF16), weights, accs, stage, pltpu.SemaphoreType.DMA],
        flops=9 * 10**9,
        name="forward",
    )

    gain, shift = (jnp.pad(gather(v).astype(F32), (0, padded - channels)) for v in (norm_gain, norm_shift))
    in_full, in_b, out_full, out_b = gather(in_proj), gather(in_bias), gather(out_proj), gather(out_bias)
    w_in = jnp.concatenate([in_full, in_b[None]], axis=0)
    w_in = jnp.pad(w_in, ((0, padded - channels - 1), (0, hidden_pad - hidden)))
    w_out = jnp.concatenate([out_full, out_b[None]], axis=0)
    w_out = jnp.pad(w_out, ((0, hidden_pad - hidden - 1), (0, padded - channels)))
    w_in_t = jnp.pad(in_full, ((0, padded - channels), (0, hidden_pad - hidden))).T
    w_out_t = w_out.T

    own_count = jnp.sum(land.astype(F32))
    stats = jnp.concatenate([stats[:2], jnp.broadcast_to(own_count, (1, padded))], axis=0)
    stats = butterfly(stats, merge_stats)
    count = jnp.maximum(stats[2, 0], 1.0)
    mean = stats[0]
    inverse = lax.rsqrt(stats[1] / count + EPSILON)
    zero = jnp.zeros_like(gain)
    vec = jnp.stack([mean, inverse, gain, shift, zero, zero, zero, zero])

    rows = 3 if height % 3 == 0 else height
    steps = height // rows
    part = rows * FINE * PAD
    by_row = lambda *rest: pl.BlockSpec((rows, *rest), lambda i: (i,) + (0,) * len(rest))
    by_cell = lambda lanes: pl.BlockSpec((part, lanes), lambda i: (i, 0))
    fixed = lambda *shape: pl.BlockSpec(shape, lambda i: (0,) * len(shape))
    output, act, ghid, gz, zvals, sums = call(
        functools.partial(pointwise_kernel, channels, hidden),
        [
            ((height, width, channels), BF16),
            ((cells, hidden_pad), BF16),
            ((cells, hidden_pad), BF16),
            (plane_shape, F32),
            ((cells, padded), BF16),
            ((8, padded), F32),
        ],
        (conv, gbranch, feats, land_t, mask, vec, w_in, w_out, w_in_t, w_out_t),
        [
            by_row(FINE, PAD, padded),
            by_row(FINE, PAD, padded),
            by_row(width, channels),
            fixed(width, height),
            by_row(FINE, PAD, LANES),
            fixed(8, padded),
            fixed(padded, hidden_pad),
            fixed(hidden_pad, padded),
            fixed(hidden_pad, padded),
            fixed(padded, hidden_pad),
        ],
        [pltpu.VMEM((rows, tile_count, round_up(FINE * PAD, 8), LANES), F32)],
        flops=14 * 10**9,
        grid=(steps,),
        out_specs=[
            by_row(width, channels),
            by_cell(hidden_pad),
            by_cell(hidden_pad),
            by_row(FINE, PAD, padded),
            by_cell(padded),
            fixed(8, padded),
        ],
        name="pointwise",
    )

    sums = butterfly(sums[:2], lambda mine, other: mine + other)
    grad_rows = round_up(channels + 1, 16)
    big = 2 * part if steps % 2 == 0 else part
    by_big = lambda lanes: pl.BlockSpec((big, lanes), lambda i: (i, 0))
    grad_in, grad_out = call(
        weight_kernel,
        [((grad_rows, hidden_pad), F32), ((grad_rows, hidden_pad), F32)],
        (zvals, ghid, gbranch.reshape(cells, padded), act),
        [by_big(padded), by_big(hidden_pad), by_big(padded), by_big(hidden_pad)],
        flops=7 * 10**9,
        grid=(cells // big,),
        out_specs=[fixed(grad_rows, hidden_pad)] * 2,
        name="weight_grads",
    )

    grad_gain, grad_shift = sums[0], sums[1]
    scaled = inverse * gain
    gvec = jnp.stack([mean, inverse, scaled, scaled * grad_shift / count, scaled * grad_gain / count, zero, zero, zero])
    tap_rows = round_up(TAPS, 8)
    gconv, grad_taps = call(
        functools.partial(gradient_kernel, channels),
        [(plane_shape, BF16), ((blocks, tap_rows, LANES), F32)],
        (gz, conv, mask, gvec, paired, top, bottom, jnp.asarray(tap_selectors(tap_rows))),
        [WHOLE] * 4 + [HBM] + [WHOLE] * 3,
        [
            pltpu.VMEM(paired_shape, BF16),
            pltpu.VMEM((blocks, block_rows, 4 * HALF), BF16),
            stage,
            pltpu.SemaphoreType.DMA,
        ],
        flops=9 * 10**9,
        name="gradient",
    )
    gtop, gbottom = rims(gconv)
    (grad_features,) = call(
        functools.partial(backward_kernel, channels),
        [((height, width, channels), BF16)],
        (gconv, gtop, gbottom, taps, mask, cot, land_t),
        [WHOLE] * 7,
        [
            pltpu.VMEM(paired_shape, BF16),
            weights,
            accs,
            pltpu.VMEM((2, round_up(FINE * PAD, 8), LANES), F32),
        ],
        flops=9 * 10**9,
        name="backward",
    )

    grad_taps = jnp.swapaxes(grad_taps[:, :TAPS, :HALF], 1, 2).reshape(blocks * HALF, TAPS)[:channels]
    grad_taps, grad_in, grad_out = lax.psum((grad_taps, grad_in, grad_out), ("dp", "fsdp"))
    return (
        output[None, None],
        grad_features[None, None],
        own_share(grad_taps),
        own_share(grad_gain[:channels]),
        own_share(grad_shift[:channels]),
        own_share(grad_in[:channels, :hidden]),
        own_share(grad_in[channels, :hidden]),
        own_share(grad_out[:channels, :hidden].T),
        own_share(grad_out[:channels, hidden]),
    )


def solution(mesh):
    spread = P("dp", "fsdp", None, None, None)
    split = P("fsdp", None)
    line = P("fsdp")
    return jax.shard_map(
        local,
        mesh=mesh,
        in_specs=(spread, P(), spread, split, line, line, split, line, split, line),
        out_specs=(spread, spread, split, line, line, split, line, split, line),
        check_vma=False,
    )
```

time: 750 us -> 332 us (0.44)
  other arithmetic: 353 us -> 10.8 us
  Pallas kernels: 0 us -> 131 us
  blocking collectives: 196 us -> 82.2 us
  local copies, waits for them, and re-layouts: 87.9 us -> 24.1 us
  matrix products: 60.6 us -> 0 us
  waiting for transfers between devices: 14.2 us -> 36 us
  starting transfers between devices: 13.3 us -> 26.6 us
    reduce_sum x10 -> x1, other arithmetic: 169 us -> 0.62 us  [local(): own_count = jnp.sum(land.astype(F32))]
    pallas_call x0 -> x6, Pallas kernels: none -> 131 us  [call(): pl.pallas_call(kernel, out_shape=[jax.ShapeDtypeStruct(shape, dtype) for...]
    psum x4 -> x1, blocking collectives: 166 us -> 51.2 us  [local(): lax.psum((grad_taps, grad_in, grad_out), ('dp', 'fsdp'))]
    concatenate x24 -> x8, other arithmetic: 100 us -> 3.4 us  [the longest x1 1.46 us: local(): jnp.concatenate([stats[:2], jnp.broadcast_to(own_count, (1, padded))], ax...]
    broadcast_in_dim x1 -> x0, other arithmetic: 72.5 us -> none  [local(): grad_features[None]]
    dot_general x6 -> x0, matrix products: 60.6 us -> none  [the longest x1 18.4 us: local(): lax.dot_general(gbranch, out_back, contract_cols, preferred_element_type=...]
    reshape x5 -> x3, local copies, waits for them, and re-layouts: 26.3 us -> 0.21 us  [the longest x2 0.12 us: local(): taps = jnp.swapaxes(taps.reshape(blocks, HALF, TAPS), 1, 2)]
    another operation x50 -> x10, local copies, waits for them, and re-layouts: 22.7 us -> 1.27 us  [the longest x6 0.64 us: local(): jnp.stack([mean, inverse, scaled, scaled * grad_shift / count, scaled * g...]
  transfers between devices with their start and end apart: 5 -> 15, of which waited for: 1 -> 8; matrix products, arithmetic and copies ran while one was open for 23% -> 5% of each run, Pallas kernels for 0% -> 22%
where the time goes in v1:
time: 332 us; the launch traced here: 328 us
  Pallas kernels  131 us (39%)
  blocking collectives  82.2 us (25%)
  waiting for transfers between devices  36 us (11%)
  starting transfers between devices  26.6 us (8%)
  local copies, waits for them, and re-layouts  24.1 us (7%)
  between operations  16.9 us (5%)
  other arithmetic  10.8 us (3%)
    pallas_call x6, Pallas kernels, call(): pl.pallas_call(kernel, out_shape=[jax.ShapeDtypeStruct(shape, dtype) for...  131 us
    psum x1, blocking collectives, local(): lax.psum((grad_taps, grad_in, grad_out), ('dp', 'fsdp'))  51.2 us
    psum x1, waiting for transfers between devices, local(): lax.psum((grad_taps, grad_in, grad_out), ('dp', 'fsdp'))  27.4 us
    all_gather x3, blocking collectives, gather(): return lax.all_gather(value, 'fsdp', axis=0, tiled=True)  23.7 us
    ppermute x10, starting transfers between devices, butterfly(): values = merge(values, lax.ppermute(values, axis, partners(size, bit)))  16.3 us
    ppermute x10, waiting for transfers between devices, butterfly(): values = merge(values, lax.ppermute(values, axis, partners(size, bit)))  8.57 us
    unnamed x44, local copies, waits for them, and re-layouts  8.34 us
    ppermute x2, starting transfers between devices, rims(): lax.ppermute(array[-SPAN:], 'dp', down)  7.44 us
  transfers between devices with their start and end apart: 15, of which 8 were waited for; matrix products, arithmetic and copies ran while one was open for 5% of the time, Pallas kernels for 22%

profile of v1, /device:TPU:0, one launch (start us, length us, event | category | flops | bytes accessed | tf_op | source)
XLA Modules:
  0.0 328.0 jit_solution(9041958117614313338)
XLA Ops:
  9.2 1.4 bitcast_multiply_fusion
  10.5 4.9 %collective-permute-start = (bf16[3,180,300]{2,1,0:T(8,128)(2,1)S(1)}, bf16[3,180,300]{2,1,0:T(8,128)(2,1)S(1)}, u32[]{:S(2)}, u32[]{:S(2)}) collective-permute-start(bf16[3,180,300]{2,1,0:T(8,128)(2,1)S(1)} %get-tuple-element.89), channel_id=1, source_target_pairs={{0,4},{4,8},{8,12},{12,16},{16,20},{20,24},{24,28},{1,5},{5,9},{9,... | collective-permute-start | bytes 972008 | tf_op jit(solution)/shard_map/ppermute | solution.py:475
  15.4 1.3 collective-permute-start.1
  16.7 5.3 %all-gather = bf16[4,75,49]{1,2,0:T(8,128)(2,1)S(1)} all-gather(bf16[1,75,49]{1,2,0:T(8,128)(2,1)S(1)} %bitcast.51), channel_id=1, replica_groups=mesh['dp'=8,'fsdp'=4] {'fsdp'}, dimensions={0}, use_global_device_ids=true | all-gather | bytes 36750 | tf_op jit(solution)/shard_map/all_gather | solution.py:497
  23.0 9.5 %all-gather.2 = bf16[4,300,300]{2,1,0:T(8,128)(2,1)S(1)} all-gather(bf16[1,300,300]{2,1,0:T(8,128)(2,1)S(1)} %bitcast.48), channel_id=1, replica_groups=mesh['dp'=8,'fsdp'=4] {'fsdp'}, dimensions={0}, use_global_device_ids=true | all-gather | bytes 900000 | tf_op jit(solution)/shard_map/all_gather | solution.py:497
  36.1 7.4 %all-reduce.11 = (bf16[300]{0:T(512)(128)(2,1)S(1)}, bf16[300]{0:T(512)(128)(2,1)S(1)}, bf16[1200]{0:T(1024)(128)(2,1)S(1)}, bf16[300]{0:T(512)(128)(2,1)S(1)}) all-reduce(bf16[300]{0:T(512)(128)(2,1)S(1)} %dynamic-update-slice, bf16[300]{0:T(512)(128)(2,1)S(1)} %dynamic-update-slice.1, ...), channel_id=1, replica_groups=mesh['dp'=8,'fsdp'=4] {'fsdp'}, use_global_device_ids=true, to_apply=%add.6 | all-reduce | flops 2100 | bytes 8400
  44.8 11.1 %prepare.1 = (bf16[5,12,9,16,256]{4,3,2,1,0:T(8,128)(2,1)}, bf16[18,12,16,384]{3,2,1,0:T(8,128)(2,1)}, f32[18,12,16,128]{3,2,1,0:T(8,128)}) custom-call(bf16[18,180,300]{2,1,0:T(8,128)(2,1)} %bitcast.41, bf16[18,180,300]{2,1,0:T(8,128)(2,1)} %bitcast.43, f32[180,18]{1,0:T(8,128)} %get-tuple-element.91.land_t), custom_call_target="tpu_custom_call" | custom-call | bytes 20971520 | tf_op jit(solution)/shard_map/prepare/pallas_call | solution.py:37
  56.7 25.6 %forward.1 = (f32[18,12,16,384]{3,2,1,0:T(8,128)}, f32[8,384]{1,0:T(8,128)}) custom-call(bf16[5,12,9,16,256]{4,3,2,1,0:T(8,128)(2,1)} %get-tuple-element.24.paired_hbm, bf16[3,180,300]{2,1,0:T(8,128)(2,1)} %copy-done.9, bf16[3,180,300]{2,1,0:T(8,128)(2,1)} %collective-permute-done.1.bottom, f32[5,49,128]{2,1,0:T(8,128)} %maximum_convert_fusion.taps, ...), custom_call_target="tpu_custom_call" | custom-call | flops 8999999488 | tf_op jit(solution)/shard_map/forward/pallas_call | solution.py:37
  82.3 1.5 slice_select_fusion
  84.9 1.4 fusion.17
  86.4 1.4 add_divide_fusion.4
  88.3 9.0 %all-gather.1 = bf16[4,75,1200]{2,1,0:T(8,128)(2,1)S(1)} all-gather(bf16[1,75,1200]{2,1,0:T(8,128)(2,1)S(1)} %bitcast.49), channel_id=1, replica_groups=mesh['dp'=8,'fsdp'=4] {'fsdp'}, dimensions={0}, use_global_device_ids=true | all-gather | bytes 900000 | tf_op jit(solution)/shard_map/all_gather | solution.py:497
  97.7 2.7 collective-permute-start.4
  102.4 2.7 collective-permute-start.5
  106.8 3.1 collective-permute-start.6
  109.9 1.3 copy.47.w_out
  113.3 32.3 %pointwise.1 = (bf16[18,180,300]{2,1,0:T(8,128)(2,1)}, bf16[3456,1280]{1,0:T(8,128)(2,1)}, bf16[3456,1280]{1,0:T(8,128)(2,1)}, f32[18,12,16,384]{3,2,1,0:T(8,128...) custom-call(f32[18,12,16,384]{3,2,1,0:T(8,128)} %get-tuple-element.26.conv, ...), custom_call_target="tpu_custom_call" | custom-call | flops 14000000000 | tf_op jit(solution)/shard_map/pointwise/pallas_call | solution.py:37
  148.2 1.4 collective-permute-start.8
  149.6 2.2 collective-permute-done.8
  152.8 2.6 collective-permute-done.9
  155.4 1.9 collective-permute-start.10
  157.3 1.7 collective-permute-done.10
  159.0 2.9 collective-permute-start.11
  161.9 12.3 %weight_grads.1 = (f32[304,1280]{1,0:T(8,128)}, f32[304,1280]{1,0:T(8,128)}) custom-call(bf16[3456,384]{1,0:T(8,128)(2,1)} %get-tuple-element.34.zvals, bf16[3456,1280]{1,0:T(8,128)(2,1)} %get-tuple-element.35.ghid, bf16[3456,384]{1,0:T(8,128)(2,1)} %bitcast.52, bf16[3456,1280]{1,0:T(8,128)(2,1)} %get-tuple-element.36.act), custom_call_target="tpu_custom_call" | custom-call | flops 7000000000 | tf_op jit(solution)/shard_map/weight_grads/pallas_call | solution.py:37
  175.0 23.2 %gradient.1 = (bf16[18,12,16,384]{3,2,1,0:T(8,128)(2,1)}, f32[5,56,128]{2,1,0:T(8,128)}) custom-call(f32[18,12,16,384]{3,2,1,0:T(8,128)} %get-tuple-element.30.gz, f32[18,12,16,384]{3,2,1,0:T(8,128)} %get-tuple-element.26.conv, f32[18,12,16,128]{3,2,1,0:T(8,128)} %get-tuple-element.25.mask, f32[8,384]{1,0:T(8,128)} %stack.41.vec, ...), custom_call_target="tpu_custom_call" | custom-call | flops 8999999488 | tf_op jit(solution)/shard_map/gradient/pallas_call | solution.py:37
  199.5 2.5 collective-permute-start.12
  202.0 1.5 collective-permute-start.13
  204.7 51.2 %psum.21 = f32[300,49]{0,1:T(8,128)S(1)} all-reduce(f32[300,49]{0,1:T(8,128)S(1)} %bitcast.45), channel_id=1, replica_groups=mesh['dp'=8,'fsdp'=4] {'dp','fsdp'}, use_global_device_ids=true, to_apply=%region_1.2 | all-reduce | flops 14700 | bytes 117600 | tf_op jit(solution)/shard_map/psum | solution.py:663
  259.2 26.9 %backward.1 = bf16[18,180,300]{2,1,0:T(8,128)(2,1)} custom-call(bf16[18,12,16,384]{3,2,1,0:T(8,128)(2,1)} %get-tuple-element.32.gconv, bf16[3,12,16,384]{3,2,1,0:T(8,128)(2,1)} %copy-done.7, bf16[3,12,16,384]{3,2,1,0:T(8,128)(2,1)} %copy-done.8, f32[5,49,128]{2,1,0:T(8,128)} %maximum_convert_fusion.taps, f32[18,12,16,128]{3,2,1,0:T(8,128)} %get-tuple-element.25.mask, ...), custom_call_target="tpu_custom_call" | custom-call | flops 8999999488 | tf_op jit(solution)/shard_map/backward/pallas_call | solution.py:37
  286.1 27.4 %all-reduce.14.cloned.1.call-done = (f32[304,1280]{1,0:T(8,128)}, f32[304,1280]{1,0:T(8,128)}) async-done(((f32[304,1280]{1,0:T(8,128)}, f32[304,1280]{1,0:T(8,128)}), (f32[304,1280]{1,0:T(8,128)}, f32[304,1280]{1,0:T(8,128)})) %all-reduce.14.cloned.1.call-update) | async-done | bytes 3112976 | tf_op jit(solution)/shard_map/psum | solution.py:663
  314.5 1.3 dynamic-slice_bitcast_fusion
  317.6 1.8 constant_dynamic-slice_fusion.1
  (123 shorter events, 28.6 us)
Async XLA Ops:
  7.2 0.9 copy-start
  7.2 9.5 %copy-start.4 = (bf16[75,49]{0,1:T(8,128)(2,1)S(1)}, bf16[75,49]{0,1:T(8,128)(2,1)}, u32[]{:S(2)}) copy-start(bf16[75,49]{0,1:T(8,128)(2,1)} %param.14) | copy-start | bytes 22054
  7.2 15.8 %copy-start.2 = (bf16[300,300]{1,0:T(8,128)(2,1)S(1)}, bf16[300,300]{1,0:T(8,128)(2,1)}, u32[]{:S(2)}) copy-start(bf16[300,300]{1,0:T(8,128)(2,1)} %param.19) | copy-start | bytes 540004
  7.2 306.3 %all-reduce.14.cloned.1.call-start = ((), (), s32[]{:S(2)}) async-start(), calls=%async_computation | async-start | bytes 6225920 | tf_op jit(solution)/shard_map/psum | solution.py:663
  9.0 24.1 %copy-start.13 = (u32[32]{0:T(128)S(1)}, u32[32]{0:T(128)}, u32[]{:S(2)}) copy-start(u32[32]{0:T(128)} %constant.79) | copy-start | bytes 388
  9.0 26.0 %copy-start.10 = (bf16[75]{0:T(256)(128)(2,1)S(1)}, bf16[75]{0:T(256)(128)(2,1)}, u32[]{:S(2)}) copy-start(bf16[75]{0:T(256)(128)(2,1)} %param.15) | copy-start | bytes 454
  9.0 26.3 %copy-start.11 = (bf16[75]{0:T(256)(128)(2,1)S(1)}, bf16[75]{0:T(256)(128)(2,1)}, u32[]{:S(2)}) copy-start(bf16[75]{0:T(256)(128)(2,1)} %param.16) | copy-start | bytes 454
  9.0 26.5 %copy-start.12 = (bf16[75]{0:T(256)(128)(2,1)S(1)}, bf16[75]{0:T(256)(128)(2,1)}, u32[]{:S(2)}) copy-start(bf16[75]{0:T(256)(128)(2,1)} %param.20) | copy-start | bytes 454
  9.1 26.8 %copy-start.5 = (bf16[300]{0:T(512)(128)(2,1)S(1)}, bf16[300]{0:T(512)(128)(2,1)}, u32[]{:S(2)}) copy-start(bf16[300]{0:T(512)(128)(2,1)} %param.18) | copy-start | bytes 1804
  10.5 45.4 %collective-permute-start = (bf16[3,180,300]{2,1,0:T(8,128)(2,1)S(1)}, bf16[3,180,300]{2,1,0:T(8,128)(2,1)S(1)}, u32[]{:S(2)}, u32[]{:S(2)}) collective-permute-start(bf16[3,180,300]{2,1,0:T(8,128)(2,1)S(1)} %get-tuple-element.89), channel_id=1, source_target_pairs={{0,4},{4,8},{8,12},{12,16},{16,20},{20,24},{24,28},{1,5},{5,9},{9,... | collective-permute-start | bytes 972008 | tf_op jit(solution)/shard_map/ppermute | solution.py:475
  15.4 40.5 %collective-permute-start.1 = (bf16[3,180,300]{2,1,0:T(8,128)(2,1)S(1)}, bf16[3,180,300]{2,1,0:T(8,128)(2,1)}, u32[]{:S(2)}, u32[]{:S(2)}) collective-permute-start(bf16[3,180,300]{2,1,0:T(8,128)(2,1)S(1)} %get-tuple-element.88), channel_id=1, source_target_pairs={{4,0},{8,4},{12,8},{16,12},{20,16},{24,20},{28,24},{5,1},{9,5},{13... | collective-permute-start | bytes 972008 | tf_op jit(solution)/shard_map/ppermute | solution.py:475
  55.9 0.8 copy-start.9
  56.7 25.6 %copy-start.6 = (pred[3]{0:T(512)(128)(4,1)S(1)}, pred[3]{0:T(512)(128)(4,1)}, u32[]{:S(2)}) copy-start(pred[3]{0:T(512)(128)(4,1)} %constant.49.clone.1) | copy-start | bytes 13
  82.3 6.1 %copy-start.3 = (bf16[75,1200]{1,0:T(8,128)(2,1)S(1)}, bf16[75,1200]{1,0:T(8,128)(2,1)}, u32[]{:S(2)}) copy-start(bf16[75,1200]{1,0:T(8,128)(2,1)} %param.17) | copy-start | bytes 540004
  83.7 1.2 collective-permute-start.2
  87.7 9.9 %collective-permute-start.3 = (f32[3,384]{1,0:T(4,128)S(1)}, f32[3,384]{1,0:T(4,128)S(1)}, u32[]{:S(2)}, u32[]{:S(2)}) collective-permute-start(f32[3,384]{1,0:T(4,128)S(1)} %pad_maximum_fusion), channel_id=1, source_target_pairs={{0,2},{1,3},{2,0},{3,1},{4,6},{5,7},{6,4},{7,5},{8,10},{9,11},{10,... | collective-permute-start | bytes 13832 | tf_op jit(solution)/shard_map/ppermute | solution.py:458
  97.7 4.6 %collective-permute-start.4 = (f32[3,384]{1,0:T(4,128)S(1)}, f32[3,384]{1,0:T(4,128)S(1)}, u32[]{:S(2)}, u32[]{:S(2)}) collective-permute-start(f32[3,384]{1,0:T(4,128)S(1)} %pad_maximum_fusion.1), channel_id=1, source_target_pairs={{0,4},{4,0},{8,12},{12,8},{16,20},{20,16},{24,28},{28,24},{1,5},{5... | collective-permute-start | bytes 13832 | tf_op jit(solution)/shard_map/ppermute | solution.py:458
  102.4 4.3 %collective-permute-start.5 = (f32[3,384]{1,0:T(4,128)S(1)}, f32[3,384]{1,0:T(4,128)S(1)}, u32[]{:S(2)}, u32[]{:S(2)}) collective-permute-start(f32[3,384]{1,0:T(4,128)S(1)} %pad_maximum_fusion.2), channel_id=1, source_target_pairs={{0,8},{4,12},{8,0},{12,4},{16,24},{20,28},{24,16},{28,20},{1,9},{5... | collective-permute-start | bytes 13832 | tf_op jit(solution)/shard_map/ppermute | solution.py:458
  106.8 4.7 %collective-permute-start.6 = (f32[3,384]{1,0:T(4,128)S(1)}, f32[3,384]{1,0:T(4,128)S(1)}, u32[]{:S(2)}, u32[]{:S(2)}) collective-permute-start(f32[3,384]{1,0:T(4,128)S(1)} %pad_maximum_fusion.3), channel_id=1, source_target_pairs={{0,16},{4,20},{8,24},{12,28},{16,0},{20,4},{24,8},{28,12},{1,17},{... | collective-permute-start | bytes 13832 | tf_op jit(solution)/shard_map/ppermute | solution.py:458
  146.3 1.2 collective-permute-start.7
  148.2 3.6 %collective-permute-start.8 = (f32[2,384]{1,0:T(2,128)S(1)}, f32[2,384]{1,0:T(2,128)S(1)}, u32[]{:S(2)}, u32[]{:S(2)}) collective-permute-start(f32[2,384]{1,0:T(2,128)S(1)} %slice_add_fusion.9), channel_id=1, source_target_pairs={{0,2},{1,3},{2,0},{3,1},{4,6},{5,7},{6,4},{7,5},{8,10},{9,11},{10,... | collective-permute-start | bytes 9224 | tf_op jit(solution)/shard_map/ppermute | solution.py:458
  151.8 3.6 %collective-permute-start.9 = (f32[2,384]{1,0:T(2,128)S(1)}, f32[2,384]{1,0:T(2,128)S(1)}, u32[]{:S(2)}, u32[]{:S(2)}) collective-permute-start(f32[2,384]{1,0:T(2,128)S(1)} %add.144), channel_id=1, source_target_pairs={{0,4},{4,0},{8,12},{12,8},{16,20},{20,16},{24,28},{28,24},{1,5},{5... | collective-permute-start | bytes 9224 | tf_op jit(solution)/shard_map/ppermute | solution.py:458
  155.4 3.6 %collective-permute-start.10 = (f32[2,384]{1,0:T(2,128)S(1)}, f32[2,384]{1,0:T(2,128)S(1)}, u32[]{:S(2)}, u32[]{:S(2)}) collective-permute-start(f32[2,384]{1,0:T(2,128)S(1)} %add.145), channel_id=1, source_target_pairs={{0,8},{4,12},{8,0},{12,4},{16,24},{20,28},{24,16},{28,20},{1,9},{5... | collective-permute-start | bytes 9224 | tf_op jit(solution)/shard_map/ppermute | solution.py:458
  159.0 15.3 %collective-permute-start.11 = (f32[2,384]{1,0:T(2,128)S(1)}, f32[2,384]{1,0:T(2,128)S(1)}, u32[]{:S(2)}, u32[]{:S(2)}) collective-permute-start(f32[2,384]{1,0:T(2,128)S(1)} %add.146), channel_id=1, source_target_pairs={{0,16},{4,20},{8,24},{12,28},{16,0},{20,4},{24,8},{28,12},{1,17},{... | collective-permute-start | bytes 9224 | tf_op jit(solution)/shard_map/ppermute | solution.py:458
  199.5 58.2 %collective-permute-start.12 = (bf16[3,12,16,384]{3,2,1,0:T(8,128)(2,1)S(1)}, bf16[3,12,16,384]{3,2,1,0:T(8,128)(2,1)S(1)}, u32[]{:S(2)}, u32[]{:S(2)}) collective-permute-start(bf16[3,12,16,384]{3,2,1,0:T(8,128)(2,1)S(1)} %get-tuple-element.87), channel_id=1, source_target_pairs={{0,4},{4,8},{8,12},{12,16},{16,20},{20,24},{24,28},{1,5},{5,9},{9,... | collective-permute-start | bytes 1327112 | tf_op jit(solution)/shard_map/ppermute | solution.py:475
  202.0 55.7 %collective-permute-start.13 = (bf16[3,12,16,384]{3,2,1,0:T(8,128)(2,1)S(1)}, bf16[3,12,16,384]{3,2,1,0:T(8,128)(2,1)S(1)}, u32[]{:S(2)}, u32[]{:S(2)}) collective-permute-start(bf16[3,12,16,384]{3,2,1,0:T(8,128)(2,1)S(1)} %get-tuple-element.86), channel_id=1, source_target_pairs={{4,0},{8,4},{12,8},{16,12},{20,16},{24,20},{28,24},{5,1},{9,5},{13... | collective-permute-start | bytes 1327112 | tf_op jit(solution)/shard_map/ppermute | solution.py:475
  257.7 0.8 copy-start.7
  258.4 0.8 copy-start.8
  259.2 61.5 %copy-start.1 = (s32[144,180]{1,0:T(8,128)S(1)}, s32[144,180]{1,0:T(8,128)}, u32[]{:S(2)}) copy-start(s32[144,180]{1,0:T(8,128)} %param.12) | copy-start | bytes 311044
Sparse Core Ops, SparseCore 0:
  174.4 139.0 all-reduce.13
